TPU v7x, 32 devices: a whole 2x2x4 slice. The times are simulated.
32 devices in a mesh: grp: 2 (over x), leaf: 16 (over z, y, core).
Axes of the slice: x: 2, y: 2, z: 4, core: 2. Of those that a mesh axis runs over, the one named last changes fastest.
Arguments:
- vectors: bfloat16 [32, 65536], P(None, ('grp', 'leaf')), parts along dimension 1, may hold values from -6 to 6
- leaf_basis: bfloat16 [512, 64, 128], P(('grp', 'leaf')), parts along dimension 0, may hold values from -0.5 to 0.5
- src_factors: bfloat16 [3, 512, 64, 128], P(None, ('grp', 'leaf')), parts along dimension 1, may hold values from -0.5 to 0.5
- src_cross: bfloat16 [512, 64, 128], P(('grp', 'leaf')), parts along dimension 0, may hold values from -0.5 to 0.5
- pair_factors: bfloat16 [4096, 64, 128], P(('grp', 'leaf')), parts along dimension 0, may hold values from -0.1875 to 0.1875
- tgt_cross: bfloat16 [512, 64, 128], P(('grp', 'leaf')), parts along dimension 0, may hold values from -0.5 to 0.5
- tgt_factors: bfloat16 [3, 512, 64, 128], P(None, ('grp', 'leaf')), parts along dimension 1, may hold values from -0.5 to 0.5
- out_basis: bfloat16 [512, 64, 128], P(('grp', 'leaf')), parts along dimension 0, may hold values from -0.75 to 0.75
- src_pairing: int32 [3, 16], replicated, may hold values from 0 to 15, as said below
- tgt_pairing: int32 [3, 16], replicated, may hold values from 0 to 15, as said below
- pair_sources: int32 [4096, 2], P(('grp', 'leaf')), parts along dimension 0, may hold values from 0 to 15
- pair_owner: int32 [4096, 1], P(('grp', 'leaf')), parts along dimension 0, may hold values from 0 to 15; in each aligned block of 128 rows (0 to 127, 128 to 255, ...) at most 16 rows name the same one
- pair_target: int32 [4096], P(('grp', 'leaf')), parts along dimension 0, may hold values from 0 to 15
Outputs:
- potentials: bfloat16 [32, 65536], P(None, ('grp', 'leaf')), parts along dimension 1
There are 2 independent parts, one for each index of `grp`. A program takes and returns all parts, laid end to end along the dimension named above; an argument that names none is the same for every part. Nothing has to cross between parts.
Inputs may be any that keep to these rules, and one draw needn't show every extreme that they name: `src_pairing`: each row pairs the 16 blocks of one device two by two: entry j names the partner of j, whose entry names j. `tgt_pairing`: each row pairs the 16 blocks of one device two by two: entry j names the partner of j, whose entry names j. `pair_owner`: among the 128 interactions of one device no owner appears more than 16 times, and some owner appears exactly 16 times.
All inputs are finite; a program needn't handle non-finite values.
Results may differ from a plain program's by a relative error of at most 0.019.
Values may be sent and summed in bfloat16 or wider, within the bound.
A program may use at most 64 MiB of HBM per device.

v0:
```python
import jax
import jax.numpy as jnp
from jax import lax
from jax.sharding import PartitionSpec as P


def partner(array, axis, stride):
    return lax.ppermute(array, axis, [(i, i ^ 1 << stride) for i in range(lax.axis_size(axis))])


def butterfly(factors, current, other):
    joined = jnp.concatenate([current, other], axis=1)
    return jnp.einsum("brk,bkv->brv", factors, joined, preferred_element_type=jnp.float32).astype(
        jnp.bfloat16
    )


def body(
    vectors,
    leaf_basis,
    src_factors,
    src_cross,
    pair_factors,
    tgt_cross,
    tgt_factors,
    out_basis,
    src_pairing,
    tgt_pairing,
    pair_sources,
    pair_owner,
    pair_target,
):
    vec_count = vectors.shape[0]
    blocks_dev = leaf_basis.shape[0]
    rank_size = leaf_basis.shape[1]
    blk_size = leaf_basis.shape[2]
    pairs_count = pair_factors.shape[0]
    devices = lax.axis_size("leaf")
    top_bit = devices.bit_length() - 2
    columns = vectors.reshape(vec_count, blocks_dev, blk_size)
    current = jnp.einsum(
        "brk,vbk->brv", leaf_basis, columns, preferred_element_type=jnp.float32
    ).astype(jnp.bfloat16)
    for depth in range(src_pairing.shape[0]):
        current = butterfly(
            src_factors[depth], current, jnp.take(current, src_pairing[depth], axis=0)
        )
    current = butterfly(src_cross, current, partner(current, "leaf", top_bit))
    joined = jnp.concatenate(
        [
            jnp.take(current, pair_sources[:, 0], axis=0),
            jnp.take(current, pair_sources[:, 1], axis=0),
        ],
        axis=1,
    )
    results = jnp.einsum(
        "prk,pkv->prv", pair_factors, joined, preferred_element_type=jnp.float32
    ).astype(jnp.bfloat16)
    results_flat = results.reshape(pairs_count, rank_size * vec_count)
    owner_dev = pair_owner[:, 0]
    target = owner_dev * blocks_dev + pair_target
    values = results_flat.astype(jnp.float32)
    summed = lax.psum_scatter(
        jax.ops.segment_sum(values, target, num_segments=blocks_dev * lax.axis_size("leaf")),
        "leaf",
        scatter_dimension=0,
        tiled=True,
    )
    middle_state = summed.astype(jnp.bfloat16).reshape(blocks_dev, rank_size, vec_count)
    current = butterfly(tgt_cross, middle_state, partner(middle_state, "leaf", 0))
    for depth in range(tgt_pairing.shape[0]):
        current = butterfly(
            tgt_factors[depth], current, jnp.take(current, tgt_pairing[depth], axis=0)
        )
    output = jnp.einsum("brv,brk->vbk", current, out_basis, preferred_element_type=jnp.float32)
    return output.reshape(vec_count, blocks_dev * blk_size).astype(jnp.bfloat16)


def solution(mesh):
    in_specs = (
        P(None, ("grp", "leaf")),
        P(("grp", "leaf"), None, None),
        P(None, ("grp", "leaf"), None, None),
        P(("grp", "leaf"), None, None),
        P(("grp", "leaf"), None, None),
        P(("grp", "leaf"), None, None),
        P(None, ("grp", "leaf"), None, None),
        P(("grp", "leaf"), None, None),
        P(),
        P(),
        P(("grp", "leaf"), None),
        P(("grp", "leaf"), None),
        P(("grp", "leaf")),
    )
    out_specs = P(None, ("grp", "leaf"))
    return jax.shard_map(body, mesh=mesh, in_specs=in_specs, out_specs=out_specs, check_vma=False)
```

profile of v0, /device:TPU:0, one launch (start us, length us, event | category | flops | bytes accessed | tf_op | source)
XLA Modules:
  0.0 116.2 jit_solution(711023387772009737)
XLA Ops:
  6.5 0.0 copy-start
  6.5 0.0 copy-start.2
  6.5 0.0 reduce-scatter.2.cloned.1.call-start
  6.5 0.9 compare_and_fusion.5
  7.4 1.2 %convolution_convert_fusion.10 = bf16[16,64,32]{1,2,0:T(8,128)(2,1)S(1)} fusion(bf16[16,64,128]{2,1,0:T(8,128)(2,1)} %param.18, bf16[32,2048]{1,0:T(8,128)(2,1)} %param.17), kind=kOutput, calls=%fused_computation.20 | convolution fusion | flops 8421376 | bytes 458752 | tf_op jit(solution)/shard_map/brk,vbk->brv/dot_general | solution.py:41
  8.7 0.0 copy-start.6
  8.7 0.0 copy-start.7
  8.7 0.0 copy-start.8
  8.7 0.0 copy-start.4
  8.7 0.6 gather_fusion
  9.3 0.1 broadcast_select_fusion.7
  9.4 1.2 %fusion = bf16[16,64,32]{1,2,0:T(8,128)(2,1)S(1)} fusion(bf16[3,16,64,128]{3,2,1,0:T(8,128)(2,1)} %param.19, bf16[16,64,32]{1,2,0:T(8,128)(2,1)S(1)} %broadcast_select_fusion.7, bf16[16,64,32]{1,2,0:T(8,128)(2,1)S(1)} %convolution_convert_fusion.10), kind=kOutput, calls=%fused_computation.21 | convolution fusion | flops 8683520 | bytes 458752 | tf_op jit(solution)/shard_map/brk,bkv->brv/dot_general | solution.py:13
  10.7 0.6 gather_fusion.1
  11.3 0.1 broadcast_select_fusion.6
  11.4 0.0 copy-done.2
  11.4 0.3 fusion.1
  11.7 0.6 gather_fusion.2
  12.3 0.1 broadcast_select_fusion.5
  12.4 0.3 fusion.2
  12.7 4.1 %collective-permute-start = (bf16[16,64,32]{1,2,0:T(8,128)(2,1)S(1)}, bf16[16,64,32]{1,2,0:T(8,128)(2,1)S(1)}, u32[]{:S(2)}, u32[]{:S(2)}) collective-permute-start(bf16[16,64,32]{1,2,0:T(8,128)(2,1)S(1)} %fusion.2), channel_id=1, source_target_pairs={{0,8},{1,9},{2,10},{3,11},{4,12},{5,13},{6,14},{7,15},{8,0},{9,1},... | collective-permute-start | bytes 196616 | tf_op jit(solution)/shard_map/ppermute | solution.py:8
  16.8 0.0 copy-done.6
  16.8 0.0 copy-done.7
  16.8 0.0 copy-done.8
  16.8 6.2 %collective-permute-done = bf16[16,64,32]{1,2,0:T(8,128)(2,1)S(1)} collective-permute-done((bf16[16,64,32]{1,2,0:T(8,128)(2,1)S(1)}, bf16[16,64,32]{1,2,0:T(8,128)(2,1)S(1)}, u32[]{:S(2)}, u32[]{:S(2)}) %collective-permute-start) | collective-permute-done | bytes 65568 | tf_op jit(solution)/shard_map/ppermute | solution.py:8
  23.1 0.0 copy-done.4
  23.1 0.3 fusion.3
  23.4 1.7 %gather_fusion.3 = bf16[128,64,32]{1,2,0:T(8,128)(2,1)} fusion(bf16[16,64,32]{1,2,0:T(8,128)(2,1)S(1)} %fusion.3, s32[1024]{0:T(1024)S(1)} %get-tuple-element.36), kind=kCustom, calls=%fused_computation.1.clone | custom fusion | bytes 1049088 | tf_op jit(solution)/shard_map/jit(_take)/gather | solution.py:51
  25.1 0.8 gather_fusion.4
  25.8 1.4 %broadcast_select_fusion.1 = bf16[128,64,32]{1,2,0:T(8,128)(2,1)S(1)} fusion(bf16[128,64,32]{1,2,0:T(8,128)(2,1)} %gather_fusion.3, pred[128]{0:T(512)(128)(4,1)S(1)} %get-tuple-element.13), kind=kLoop, calls=%fused_computation.35 | loop fusion | flops 262144 | bytes 1048704 | tf_op jit(solution)/shard_map/jit(_take)/select_n | solution.py:51
  27.3 0.2 broadcast_select_fusion
  27.5 0.0 copy-done
  27.5 2.6 %convert_bitcast_fusion = f32[128,64,32]{1,2,0:T(8,128)} fusion(bf16[128,64,128]{2,1,0:T(8,128)(2,1)S(1)} %copy-done, bf16[128,64,32]{1,2,0:T(8,128)(2,1)S(1)} %broadcast_select_fusion, bf16[128,64,32]{1,2,0:T(8,128)(2,1)S(1)} %broadcast_select_fusion.1), kind=kOutput, calls=%fused_computation.9 | convolution fusion | flops 69730304 | bytes 4194304 | tf_op jit(solution)/shard_map/prk,pkv->prv/dot_general | solution.py:56
  30.1 3.0 %copy.21 = f32[128,64,32]{0,2,1:T(8,128)S(1)} copy(f32[128,64,32]{1,2,0:T(8,128)} %convert_bitcast_fusion) | data formatting | bytes 2097152 | tf_op jit(solution)/shard_map/convert_element_type | solution.py:62
  33.1 1.3 %copy.22 = f32[128,2048]{1,0:T(8,128)} copy(f32[128,2048]{0,1:T(8,128)S(1)} %bitcast.80) | data formatting | bytes 2097152 | tf_op jit(solution)/shard_map/convert_element_type | solution.py:62
  34.4 0.0 copy-start.5
  34.4 4.3 %scatter_custom_fusion = f32[256,2048]{1,0:T(8,128)} fusion(s32[128]{0:T(128)S(1)} %bitcast_add_fusion, f32[128,2048]{1,0:T(8,128)} %copy.22, f32[]{:T(128)} %constant.18.clone.1), kind=kCustom, calls=%fused_computation.32 | custom fusion | flops 262144 | bytes 2097664 | tf_op jit(solution)/shard_map/scatter-add | solution.py:64
  38.7 0.0 copy-start.1
  38.7 0.0 reduce-scatter.2.cloned.1.call-update
  38.7 0.0 copy-done.5
  38.8 62.9 %reduce-scatter.2.cloned.1.call-done = f32[16,2048]{1,0:T(8,128)} async-done(((f32[256,2048]{1,0:T(8,128)}), f32[16,2048]{1,0:T(8,128)}) %reduce-scatter.2.cloned.1.call-update) | async-done | bytes 131088 | tf_op jit(solution)/shard_map/reduce_scatter | solution.py:63
  101.6 0.9 convert_element_type.87
  102.6 0.2 reshape.24
  102.7 0.1 copy.24
  102.9 0.1 collective-permute-start.1
  103.0 0.0 copy-start.3
  103.0 1.3 %collective-permute-done.1 = bf16[16,64,32]{1,2,0:T(8,128)(2,1)S(1)} collective-permute-done((bf16[16,64,32]{1,2,0:T(8,128)(2,1)S(1)}, bf16[16,64,32]{1,2,0:T(8,128)(2,1)S(1)}, u32[]{:S(2)}, u32[]{:S(2)}) %collective-permute-start.1) | collective-permute-done | bytes 65568 | tf_op jit(solution)/shard_map/ppermute | solution.py:8
  104.3 1.2 %fusion.4 = bf16[16,64,32]{1,2,0:T(8,128)(2,1)S(1)} fusion(bf16[16,64,128]{2,1,0:T(8,128)(2,1)} %param.22, bf16[16,64,32]{1,2,0:T(8,128)(2,1)S(1)} %collective-permute-done.1, bf16[16,64,32]{1,2,0:T(8,128)(2,1)S(1)} %copy.24), kind=kOutput, calls=%fused_computation.25 | convolution fusion | flops 8683520 | bytes 458752 | tf_op jit(solution)/shard_map/brk,bkv->brv/dot_general | solution.py:13
  105.6 0.6 gather_fusion.5
  106.2 0.1 broadcast_select_fusion.4
  106.2 0.0 copy-done.1
  106.3 0.3 fusion.5
  106.6 0.6 gather_fusion.6
  107.2 0.1 broadcast_select_fusion.3
  107.2 0.3 fusion.6
  107.6 0.6 gather_fusion.7
  108.1 0.1 broadcast_select_fusion.2
  108.2 0.0 copy-done.3
  108.3 0.4 fusion.7
  108.7 0.7 copy.33
  (8 shorter events, 0.1 us)
Async XLA Ops:
  6.5 20.9 %copy-start = (bf16[128,64,128]{2,1,0:T(8,128)(2,1)S(1)}, bf16[128,64,128]{2,1,0:T(8,128)(2,1)}, u32[]{:S(2)}) copy-start(bf16[128,64,128]{2,1,0:T(8,128)(2,1)} %param.21) | copy-start | bytes 6291460
  6.5 4.8 %copy-start.2 = (bf16[3,16,64,128]{3,2,1,0:T(8,128)(2,1)S(1)}, bf16[3,16,64,128]{3,2,1,0:T(8,128)(2,1)}, u32[]{:S(2)}) copy-start(bf16[3,16,64,128]{3,2,1,0:T(8,128)(2,1)} %param.19) | copy-start | bytes 2359300
  6.5 95.1 %reduce-scatter.2.cloned.1.call-start = ((), (), s32[]{:S(2)}) async-start(), calls=%async_computation.1 | async-start | bytes 2228224 | tf_op jit(solution)/shard_map/reduce_scatter | solution.py:63
  8.7 8.1 %copy-start.6 = (s32[128,2]{0,1:T(2,128)S(1)}, s32[128,2]{0,1:T(2,128)}, u32[]{:S(2)}) copy-start(s32[128,2]{0,1:T(2,128)} %param.27) | copy-start | bytes 3076
  8.7 8.1 %copy-start.7 = (s32[128]{0:T(128)S(1)}, s32[128]{0:T(128)}, u32[]{:S(2)}) copy-start(s32[128]{0:T(128)} %param.29) | copy-start | bytes 1540
  8.7 8.1 %copy-start.8 = (s32[128,1]{0,1:T(1,128)S(1)}, s32[128,1]{0,1:T(1,128)}, u32[]{:S(2)}) copy-start(s32[128,1]{0,1:T(1,128)} %param.28) | copy-start | bytes 1540
  8.7 14.4 %copy-start.4 = (bf16[16,64,128]{2,1,0:T(8,128)(2,1)S(1)}, bf16[16,64,128]{2,1,0:T(8,128)(2,1)}, u32[]{:S(2)}) copy-start(bf16[16,64,128]{2,1,0:T(8,128)(2,1)} %param.20) | copy-start | bytes 786436
  12.7 10.4 %collective-permute-start = (bf16[16,64,32]{1,2,0:T(8,128)(2,1)S(1)}, bf16[16,64,32]{1,2,0:T(8,128)(2,1)S(1)}, u32[]{:S(2)}, u32[]{:S(2)}) collective-permute-start(bf16[16,64,32]{1,2,0:T(8,128)(2,1)S(1)} %fusion.2), channel_id=1, source_target_pairs={{0,8},{1,9},{2,10},{3,11},{4,12},{5,13},{6,14},{7,15},{8,0},{9,1},... | collective-permute-start | bytes 196616 | tf_op jit(solution)/shard_map/ppermute | solution.py:8
  34.4 4.3 %copy-start.5 = (s32[3,16]{1,0:T(4,128)S(1)}, s32[3,16]{1,0:T(4,128)}, u32[]{:S(2)}) copy-start(s32[3,16]{1,0:T(4,128)} %param.26) | copy-start | bytes 580
  38.7 67.6 %copy-start.1 = (bf16[3,16,64,128]{3,2,1,0:T(8,128)(2,1)S(1)}, bf16[3,16,64,128]{3,2,1,0:T(8,128)(2,1)}, u32[]{:S(2)}) copy-start(bf16[3,16,64,128]{3,2,1,0:T(8,128)(2,1)} %param.23) | copy-start | bytes 2359300
  102.9 1.4 %collective-permute-start.1 = (bf16[16,64,32]{1,2,0:T(8,128)(2,1)S(1)}, bf16[16,64,32]{1,2,0:T(8,128)(2,1)S(1)}, u32[]{:S(2)}, u32[]{:S(2)}) collective-permute-start(bf16[16,64,32]{1,2,0:T(8,128)(2,1)S(1)} %copy.24), channel_id=1, source_target_pairs={{0,1},{1,0},{2,3},{3,2},{4,5},{5,4},{6,7},{7,6},{8,9},{9,8},{10,11... | collective-permute-start | bytes 196616 | tf_op jit(solution)/shard_map/ppermute | solution.py:8
  103.0 5.3 %copy-start.3 = (bf16[16,64,128]{2,1,0:T(8,128)(2,1)S(1)}, bf16[16,64,128]{2,1,0:T(8,128)(2,1)}, u32[]{:S(2)}) copy-start(bf16[16,64,128]{2,1,0:T(8,128)(2,1)} %param.24) | copy-start | bytes 786436
Sparse Core Ops, SparseCore 0:
  38.8 62.7 reduce-scatter.1
where the time goes:
time: 117 us; the launch traced here: 116 us
  waiting for transfers between devices  70.4 us (60%)
  between operations  13.7 us (12%)
  local copies, waits for them, and re-layouts  11.3 us (10%)
  matrix products  8.27 us (7%)
  other arithmetic  8.25 us (7%)
  starting transfers between devices  4.17 us (4%)
    reduce_scatter x1, waiting for transfers between devices, body(): lax.psum_scatter(jax.ops.segment_sum(values, target, num_segments=blocks_...  62.9 us
    ppermute x2, waiting for transfers between devices, partner(): lax.ppermute(array, axis, [(i, i ^ 1 << stride) for i in range(lax.axis_s...  7.55 us
    convert_element_type x2, local copies, waits for them, and re-layouts, body(): values = results_flat.astype(jnp.float32)  4.32 us
    scatter-add x1, other arithmetic, body(): jax.ops.segment_sum(values, target, num_segments=blocks_dev * lax.axis_si...  4.25 us
    ppermute x2, starting transfers between devices, partner(): lax.ppermute(array, axis, [(i, i ^ 1 << stride) for i in range(lax.axis_s...  4.17 us
    dot_general x7, matrix products, butterfly(): jnp.einsum('brk,bkv->brv', factors, joined, preferred_element_type=jnp.fl...  4 us
    dot_general x1, matrix products, body(): jnp.einsum('prk,pkv->prv', pair_factors, joined, preferred_element_type=j...  2.61 us
  transfers between devices with their start and end apart: 3, of which 3 were waited for; matrix products, arithmetic and copies ran while one was open for 0% of the time, Pallas kernels for 0%

commit v1 on v0

v1 whole, which is shorter than its diff:
```python
import functools

import jax
import jax.numpy as jnp
from jax import lax
from jax.experimental import pallas as pl
from jax.experimental.pallas import tpu as pltpu
from jax.sharding import PartitionSpec as P

BF16 = jnp.bfloat16
F32 = jnp.float32
I32 = jnp.int32
NT = (((1,), (1,)), ((), ()))


def bit_of(number, bit):
    return (number // (1 << bit)) % 2


def flip(number, bit):
    return number + (1 << bit) - 2 * (1 << bit) * bit_of(number, bit)


def kernel(
    devices,
    order_of_bits,
    src_pair,
    tgt_pair,
    sources,
    owner,
    target,
    vectors_hbm,
    leaf_hbm,
    src_hbm,
    src_cross_hbm,
    pair_hbm,
    tgt_cross_hbm,
    tgt_hbm,
    out_basis_hbm,
    out_ref,
    vectors,
    leaf,
    src,
    src_cross,
    pair,
    tgt_cross,
    tgt,
    out_basis,
    state_a,
    state_b,
    packed,
    cross_in,
    near_in,
    table_vmem,
    table,
    running,
    dense,
    arrived,
    load_sem,
    table_sem,
    send_sem,
    recv_sem,
):
    me = lax.axis_index("leaf")
    bits = len(order_of_bits)
    blocks = leaf.shape[0]
    halves = blocks // 2
    pairs = pair.shape[0]
    levels = src.shape[0]
    rank = leaf.shape[1]
    vec = vectors.shape[0]
    width = 2 * rank

    loads = [
        pltpu.make_async_copy(hbm, ref, load_sem.at[i])
        for i, (hbm, ref) in enumerate(
            [
                (vectors_hbm, vectors),
                (leaf_hbm, leaf),
                (src_hbm, src),
                (src_cross_hbm, src_cross),
                (pair_hbm, pair),
                (tgt_cross_hbm, tgt_cross),
                (tgt_hbm, tgt),
                (out_basis_hbm, out_basis),
            ]
        )
    ]
    for load in loads:
        load.start()

    barrier = pltpu.get_barrier_semaphore()
    for bit in range(bits):
        pl.semaphore_signal(
            barrier,
            inc=1,
            device_id={"leaf": flip(me, bit)},
            device_id_type=pl.DeviceIdType.MESH,
        )

    def send(source, destination, bit, slot):
        return pltpu.make_async_remote_copy(
            src_ref=source,
            dst_ref=destination,
            send_sem=send_sem.at[slot],
            recv_sem=recv_sem.at[slot],
            device_id={"leaf": flip(me, bit)},
            device_id_type=pl.DeviceIdType.MESH,
        )

    low = lax.broadcasted_iota(I32, (vec, width), 1) < rank

    def twice(x, factor):
        both = jnp.concatenate([factor, factor], axis=0)
        return lax.dot_general(x, both, NT, preferred_element_type=F32)

    def local_level(factors, depth, pairing, old, new):
        for b in range(blocks):
            x = jnp.where(low, old[b], old[pairing[depth, b]])
            new[b] = twice(x, factors[depth, b]).astype(BF16)

    def cross_level(factors, own, other, new):
        for b in range(blocks):
            if b % 2 == 0:
                x = jnp.where(low, other[b // 2], own[b])
                x = jnp.concatenate([x[:, rank:], x[:, :rank]], axis=1)
            else:
                x = jnp.where(low, own[b], other[b // 2])
            new[b] = twice(x, factors[b]).astype(BF16)

    loads[0].wait()
    loads[1].wait()
    points = leaf.shape[2]
    for b in range(blocks):
        state_a[b] = twice(vectors[:, b * points : (b + 1) * points], leaf[b]).astype(BF16)
    loads[2].wait()
    now, later = state_a, state_b
    for depth in range(levels):
        local_level(src, depth, src_pair, now, later)
        now, later = later, now

    for j in range(halves):
        packed[j] = jnp.where(low, now[2 * j], now[2 * j + 1])
    pl.semaphore_wait(barrier, bits)
    cross = send(packed, cross_in, bits - 1, 0)
    cross.start()

    count_shape = (pairs, pairs)
    item = lax.broadcasted_iota(I32, count_shape, 0)
    lane = lax.broadcasted_iota(I32, count_shape, 1)
    key = jnp.broadcast_to(owner[...] * blocks + target[...], count_shape)
    first = jnp.broadcast_to(sources[:, 0:1], count_shape)
    second = jnp.broadcast_to(sources[:, 1:2], count_shape)
    key_row = jnp.sum(jnp.where(item == lane, key, 0), axis=0, keepdims=True)
    before = jnp.where((key_row == key) & (lane < item), 1, 0)
    smaller = jnp.where(key_row < key, 1, 0)
    place = jnp.sum(before + smaller, axis=1, keepdims=True)
    follows = jnp.minimum(jnp.sum(before, axis=1, keepdims=True), 1)
    sits = place == lane
    rows = [
        jnp.sum(jnp.where(sits, value, 0), axis=0, keepdims=True)
        for value in (item, first, second, jnp.broadcast_to(follows, count_shape))
    ]
    for r in range(4):
        table_vmem[r : r + 1, :] = rows[r]
    for r in range(devices * blocks // pairs):
        spot = lane + r * pairs
        upto = jnp.sum(jnp.where(key <= spot, 1, 0), axis=0, keepdims=True)
        under = jnp.sum(jnp.where(key < spot, 1, 0), axis=0, keepdims=True)
        table_vmem[4 + r : 5 + r, :] = jnp.where(upto > under, upto - 1, pairs)
    for r in range(4 + devices * blocks // pairs, table_vmem.shape[0]):
        table_vmem[r : r + 1, :] = jnp.zeros((1, pairs), I32)
    to_scalars = pltpu.make_async_copy(table_vmem, table, table_sem)
    to_scalars.start()
    running[pairs] = jnp.zeros((vec, width), BF16)
    loads[3].wait()
    loads[4].wait()
    to_scalars.wait()

    cross.wait()
    cross_level(src_cross, now, cross_in, later)
    now, later = later, now

    group = 16

    def interactions(step, total):
        for k in range(group):
            i = step * group + k
            x = jnp.where(low, now[table[1, i]], now[table[2, i]])
            c = twice(x, pair[table[0, i]]).astype(BF16).astype(F32)
            total = total * table[3, i].astype(F32) + c
            running[i] = total.astype(BF16)
        return total

    lax.fori_loop(0, pairs // group, interactions, jnp.zeros((vec, width), F32))

    def place_owner(position, carry):
        who = 0
        for s, bit in enumerate(order_of_bits):
            away = bit_of(position, bits - 1 - s)
            who = who + ((bit_of(me, bit) + away) % 2) * (1 << bit)
        start = who * blocks
        row = 4 + start // pairs
        column = start % pairs
        for j in range(halves):
            one = running[table[row, column + 2 * j]]
            two = running[table[row, column + 2 * j + 1]]
            dense[position * halves + j] = jnp.where(low, one, two)
        return carry

    lax.fori_loop(0, devices, place_owner, 0)

    unit = 8
    for s, bit in enumerate(order_of_bits):
        size = (devices >> (s + 1)) * halves
        part = arrived.at[size : 2 * size]
        move = send(dense.at[size : 2 * size], part, bit, 1 + s)
        move.start()
        move.wait()

        def add(step, carry):
            for u in range(unit):
                k = step * unit + u
                dense[k] = (dense[k].astype(F32) + arrived[size + k].astype(F32)).astype(BF16)
            return carry

        lax.fori_loop(0, size // unit, add, 0)

    near = send(dense.at[0:halves], near_in, 0, 1 + bits)
    near.start()
    for j in range(halves):
        x = dense[j]
        later[2 * j] = jnp.concatenate([x[:, :rank], x[:, :rank]], axis=1)
        later[2 * j + 1] = jnp.concatenate([x[:, rank:], x[:, rank:]], axis=1)
    now, later = later, now
    loads[5].wait()
    loads[6].wait()
    loads[7].wait()
    near.wait()
    cross_level(tgt_cross, now, near_in, later)
    now, later = later, now
    for depth in range(levels):
        local_level(tgt, depth, tgt_pair, now, later)
        now, later = later, now
    for b in range(blocks):
        y = jnp.dot(now[b][:, :rank], out_basis[b], preferred_element_type=F32)
        out_ref[:, b * points : (b + 1) * points] = y.astype(BF16)


def body(
    devices,
    vectors,
    leaf_basis,
    src_factors,
    src_cross,
    pair_factors,
    tgt_cross,
    tgt_factors,
    out_basis,
    src_pairing,
    tgt_pairing,
    pair_sources,
    pair_owner,
    pair_target,
):
    vec = vectors.shape[0]
    blocks, rank, _ = leaf_basis.shape
    pairs = pair_factors.shape[0]
    bits = devices.bit_length() - 1
    halves = blocks // 2
    width = 2 * rank
    rows = 4 + devices * blocks // pairs
    rows = -(-rows // 8) * 8
    big = [
        vectors,
        leaf_basis,
        src_factors,
        src_cross,
        pair_factors,
        tgt_cross,
        tgt_factors,
        out_basis,
    ]
    vmem = pl.BlockSpec(memory_space=pltpu.VMEM)
    smem = pl.BlockSpec(memory_space=pltpu.SMEM)
    hbm = pl.BlockSpec(memory_space=pl.ANY)
    return pl.pallas_call(
        functools.partial(kernel, devices, tuple(range(bits))),
        out_shape=jax.ShapeDtypeStruct(vectors.shape, BF16),
        in_specs=[smem, smem, vmem, vmem, vmem] + [hbm] * len(big),
        out_specs=vmem,
        scratch_shapes=[pltpu.VMEM(a.shape, a.dtype) for a in big]
        + [
            pltpu.VMEM((blocks, vec, width), BF16),
            pltpu.VMEM((blocks, vec, width), BF16),
            pltpu.VMEM((halves, vec, width), BF16),
            pltpu.VMEM((halves, vec, width), BF16),
            pltpu.VMEM((halves, vec, width), BF16),
            pltpu.VMEM((rows, pairs), I32),
            pltpu.SMEM((rows, pairs), I32),
            pltpu.VMEM((pairs + 1, vec, width), BF16),
            pltpu.VMEM((devices * halves, vec, width), BF16),
            pltpu.VMEM((devices * halves, vec, width), BF16),
            pltpu.SemaphoreType.DMA((len(big),)),
            pltpu.SemaphoreType.DMA,
            pltpu.SemaphoreType.DMA((2 + bits,)),
            pltpu.SemaphoreType.DMA((2 + bits,)),
        ],
        compiler_params=pltpu.CompilerParams(
            collective_id=0, has_side_effects=True, vmem_limit_bytes=48 * 1024 * 1024
        ),
    )(
        src_pairing,
        tgt_pairing,
        pair_sources,
        pair_owner,
        pair_target.reshape(pairs, 1),
        *big,
    )


def solution(mesh):
    in_specs = (
        P(None, ("grp", "leaf")),
        P(("grp", "leaf"), None, None),
        P(None, ("grp", "leaf"), None, None),
        P(("grp", "leaf"), None, None),
        P(("grp", "leaf"), None, None),
        P(("grp", "leaf"), None, None),
        P(None, ("grp", "leaf"), None, None),
        P(("grp", "leaf"), None, None),
        P(),
        P(),
        P(("grp", "leaf"), None),
        P(("grp", "leaf"), None),
        P(("grp", "leaf")),
    )
    out_specs = P(None, ("grp", "leaf"))
    return jax.shard_map(
        functools.partial(body, mesh.shape["leaf"]),
        mesh=mesh,
        in_specs=in_specs,
        out_specs=out_specs,
        check_vma=False,
    )
```

time: 117 us -> 49.9 us (0.43)
  waiting for transfers between devices: 70.4 us -> 0 us
  Pallas kernels: 0 us -> 36.5 us
  between operations: 13.7 us -> 0.03 us
  matrix products: 8.27 us -> 0 us
  other arithmetic: 8.25 us -> 0 us
  starting transfers between devices: 4.17 us -> 0 us
  local copies, waits for them, and re-layouts: 11.3 us -> 12.9 us
    reduce_scatter x1 -> x0, waiting for transfers between devices: 62.9 us -> none  [body(): lax.psum_scatter(jax.ops.segment_sum(values, target, num_segments=blocks_...]
    pallas_call x0 -> x1, Pallas kernels: none -> 36.5 us  [body(): pl.pallas_call(functools.partial(kernel, devices, tuple(range(bits))), ou...]
    unnamed x18 -> x23, local copies, waits for them, and re-layouts: 0.05 us -> 12.1 us
    dot_general x10 -> x0, matrix products: 8.27 us -> none  [the longest x7 4 us: butterfly(): jnp.einsum('brk,bkv->brv', factors, joined, preferred_element_type=jnp.fl...]
    ppermute x2 -> x0, waiting for transfers between devices: 7.55 us -> none  [partner(): lax.ppermute(array, axis, [(i, i ^ 1 << stride) for i in range(lax.axis_s...]
    gather x8 -> x0, local copies, waits for them, and re-layouts: 5.93 us -> none  [the longest x3 1.75 us: body(): jnp.take(current, tgt_pairing[depth], axis=0)]
    convert_element_type x3 -> x0, local copies, waits for them, and re-layouts: 5.01 us -> none  [the longest x2 4.32 us: body(): values = results_flat.astype(jnp.float32)]
    scatter-add x1 -> x0, other arithmetic: 4.25 us -> none  [body(): jax.ops.segment_sum(values, target, num_segments=blocks_dev * lax.axis_si...]
  transfers between devices with their start and end apart: 3 -> 0, of which waited for: 3 -> 0; matrix products, arithmetic and copies ran while one was open for 0% -> 0% of each run, Pallas kernels for 0% -> 0%
where the time goes in v1:
time: 49.9 us; the launch traced here: 49.4 us
  Pallas kernels  36.5 us (73%)
  local copies, waits for them, and re-layouts  12.9 us (26%)
    pallas_call x1, Pallas kernels, body(): pl.pallas_call(functools.partial(kernel, devices, tuple(range(bits))), ou...  36.5 us
    unnamed x23, local copies, waits for them, and re-layouts  12.1 us

profile of v1, /device:TPU:0, one launch (start us, length us, event | category | flops | bytes accessed | tf_op | source)
XLA Modules:
  0.0 49.4 jit_solution(6340491788145598404)
XLA Ops:
  0.0 0.8 %copy.14.sources = s32[128,2]{1,0:T(8,128)S(1)} copy(s32[128,2]{0,1:T(2,128)} %param.23) | data formatting | bytes 2048 | tf_op args[10]
  0.8 0.8 %copy.15.owner = s32[128,1]{1,0:T(8,128)S(1)} copy(s32[128,1]{0,1:T(1,128)} %param.24) | data formatting | bytes 1024 | tf_op args[11]
  1.5 0.8 %copy.16.target = s32[128,1]{1,0:T(8,128)S(1)} copy(s32[128,1]{0,1:T(1,128)} %bitcast.1) | data formatting | bytes 1024 | tf_op jit(solution)/shard_map/reshape | solution.py:317
  2.3 0.0 copy-start
  2.3 1.6 %copy-done = bf16[128,64,128]{2,1,0:T(8,128)(2,1)S(1)} copy-done((bf16[128,64,128]{2,1,0:T(8,128)(2,1)S(1)}, bf16[128,64,128]{2,1,0:T(8,128)(2,1)}, u32[]{:S(2)}) %copy-start) | copy-done | bytes 2097176
  3.9 0.0 copy-start.1
  3.9 1.1 %copy-done.1 = bf16[3,16,64,128]{3,2,1,0:T(8,128)(2,1)S(1)} copy-done((bf16[3,16,64,128]{3,2,1,0:T(8,128)(2,1)S(1)}, bf16[3,16,64,128]{3,2,1,0:T(8,128)(2,1)}, u32[]{:S(2)}) %copy-start.1) | copy-done | bytes 786456
  5.0 0.0 copy-start.2
  5.0 1.1 %copy-done.2 = bf16[3,16,64,128]{3,2,1,0:T(8,128)(2,1)S(1)} copy-done((bf16[3,16,64,128]{3,2,1,0:T(8,128)(2,1)S(1)}, bf16[3,16,64,128]{3,2,1,0:T(8,128)(2,1)}, u32[]{:S(2)}) %copy-start.2) | copy-done | bytes 786456
  6.2 0.0 copy-start.3
  6.2 0.9 %copy-done.3 = bf16[16,64,128]{2,1,0:T(8,128)(2,1)S(1)} copy-done((bf16[16,64,128]{2,1,0:T(8,128)(2,1)S(1)}, bf16[16,64,128]{2,1,0:T(8,128)(2,1)}, u32[]{:S(2)}) %copy-start.3) | copy-done | bytes 262168
  7.1 0.0 copy-start.4
  7.1 0.9 %copy-done.4 = bf16[16,64,128]{2,1,0:T(8,128)(2,1)S(1)} copy-done((bf16[16,64,128]{2,1,0:T(8,128)(2,1)S(1)}, bf16[16,64,128]{2,1,0:T(8,128)(2,1)}, u32[]{:S(2)}) %copy-start.4) | copy-done | bytes 262168
  8.1 0.0 copy-start.5
  8.1 0.9 %copy-done.5 = bf16[16,64,128]{2,1,0:T(8,128)(2,1)S(1)} copy-done((bf16[16,64,128]{2,1,0:T(8,128)(2,1)S(1)}, bf16[16,64,128]{2,1,0:T(8,128)(2,1)}, u32[]{:S(2)}) %copy-start.5) | copy-done | bytes 262168
  9.0 0.0 copy-start.6
  9.0 0.9 %copy-done.6 = bf16[16,64,128]{2,1,0:T(8,128)(2,1)S(1)} copy-done((bf16[16,64,128]{2,1,0:T(8,128)(2,1)S(1)}, bf16[16,64,128]{2,1,0:T(8,128)(2,1)}, u32[]{:S(2)}) %copy-start.6) | copy-done | bytes 262168
  10.0 0.0 copy-start.7
  10.0 0.9 %copy-done.7 = bf16[32,2048]{1,0:T(8,128)(2,1)S(1)} copy-done((bf16[32,2048]{1,0:T(8,128)(2,1)S(1)}, bf16[32,2048]{1,0:T(8,128)(2,1)}, u32[]{:S(2)}) %copy-start.7) | copy-done | bytes 131096
  10.9 0.0 copy-start.8
  10.9 0.7 %copy-done.8 = s32[3,16]{1,0:T(4,128)S(1)} copy-done((s32[3,16]{1,0:T(4,128)S(1)}, s32[3,16]{1,0:T(4,128)}, u32[]{:S(2)}) %copy-start.8) | copy-done | bytes 216
  11.6 0.0 copy-start.9
  11.6 0.7 %copy-done.9 = s32[3,16]{1,0:T(4,128)S(1)} copy-done((s32[3,16]{1,0:T(4,128)S(1)}, s32[3,16]{1,0:T(4,128)}, u32[]{:S(2)}) %copy-start.9) | copy-done | bytes 216
  12.2 36.5 %shard_map.127 = bf16[32,2048]{1,0:T(8,128)(2,1)S(1)} custom-call(s32[3,16]{1,0:T(4,128)S(1)} %copy-done.8, s32[3,16]{1,0:T(4,128)S(1)} %copy-done.9, s32[128,2]{1,0:T(8,128)S(1)} %copy.14.sources, s32[128,1]{1,0:T(8,128)S(1)} %copy.15.owner, s32[128,1]{1,0:T(8,128)S(1)} %copy.16.target, bf16[32,2048]{1,0:T(8,128)(2,1)S(1)} %copy-done.7, ...), custom_call_target="tpu_custom_call" | custom-call | tf_op jit(solution)/shard_map/pallas_call | solution.py:287
  48.8 0.7 %copy.18 = bf16[32,2048]{1,0:T(8,128)(2,1)} copy(bf16[32,2048]{1,0:T(8,128)(2,1)S(1)} %shard_map.127) | data formatting | bytes 262144
Async XLA Ops:
  2.3 1.6 %copy-start = (bf16[128,64,128]{2,1,0:T(8,128)(2,1)S(1)}, bf16[128,64,128]{2,1,0:T(8,128)(2,1)}, u32[]{:S(2)}) copy-start(bf16[128,64,128]{2,1,0:T(8,128)(2,1)} %pair_hbm.1) | copy-start | bytes 6291460
  3.9 1.1 %copy-start.1 = (bf16[3,16,64,128]{3,2,1,0:T(8,128)(2,1)S(1)}, bf16[3,16,64,128]{3,2,1,0:T(8,128)(2,1)}, u32[]{:S(2)}) copy-start(bf16[3,16,64,128]{3,2,1,0:T(8,128)(2,1)} %src_hbm.1) | copy-start | bytes 2359300
  5.0 1.1 %copy-start.2 = (bf16[3,16,64,128]{3,2,1,0:T(8,128)(2,1)S(1)}, bf16[3,16,64,128]{3,2,1,0:T(8,128)(2,1)}, u32[]{:S(2)}) copy-start(bf16[3,16,64,128]{3,2,1,0:T(8,128)(2,1)} %tgt_hbm.1) | copy-start | bytes 2359300
  6.2 0.9 %copy-start.3 = (bf16[16,64,128]{2,1,0:T(8,128)(2,1)S(1)}, bf16[16,64,128]{2,1,0:T(8,128)(2,1)}, u32[]{:S(2)}) copy-start(bf16[16,64,128]{2,1,0:T(8,128)(2,1)} %leaf_hbm.1) | copy-start | bytes 786436
  7.1 0.9 %copy-start.4 = (bf16[16,64,128]{2,1,0:T(8,128)(2,1)S(1)}, bf16[16,64,128]{2,1,0:T(8,128)(2,1)}, u32[]{:S(2)}) copy-start(bf16[16,64,128]{2,1,0:T(8,128)(2,1)} %src_cross_hbm.1) | copy-start | bytes 786436
  8.1 0.9 %copy-start.5 = (bf16[16,64,128]{2,1,0:T(8,128)(2,1)S(1)}, bf16[16,64,128]{2,1,0:T(8,128)(2,1)}, u32[]{:S(2)}) copy-start(bf16[16,64,128]{2,1,0:T(8,128)(2,1)} %tgt_cross_hbm.1) | copy-start | bytes 786436
  9.0 0.9 %copy-start.6 = (bf16[16,64,128]{2,1,0:T(8,128)(2,1)S(1)}, bf16[16,64,128]{2,1,0:T(8,128)(2,1)}, u32[]{:S(2)}) copy-start(bf16[16,64,128]{2,1,0:T(8,128)(2,1)} %out_basis_hbm.1) | copy-start | bytes 786436
  10.0 0.9 %copy-start.7 = (bf16[32,2048]{1,0:T(8,128)(2,1)S(1)}, bf16[32,2048]{1,0:T(8,128)(2,1)}, u32[]{:S(2)}) copy-start(bf16[32,2048]{1,0:T(8,128)(2,1)} %vectors_hbm.1) | copy-start | bytes 393220
  10.9 0.7 %copy-start.8 = (s32[3,16]{1,0:T(4,128)S(1)}, s32[3,16]{1,0:T(4,128)}, u32[]{:S(2)}) copy-start(s32[3,16]{1,0:T(4,128)} %src_pair.1) | copy-start | bytes 580
  11.6 0.7 %copy-start.9 = (s32[3,16]{1,0:T(4,128)S(1)}, s32[3,16]{1,0:T(4,128)}, u32[]{:S(2)}) copy-start(s32[3,16]{1,0:T(4,128)} %tgt_pair.1) | copy-start | bytes 580

commit v2 on v1

--- a/solution.py
+++ b/solution.py
@@ -23,12 +23,12 @@
 
 def kernel(
     devices,
-    order_of_bits,
-    src_pair,
-    tgt_pair,
-    sources,
-    owner,
-    target,
+    orders,
+    src_pair_hbm,
+    tgt_pair_hbm,
+    sources_hbm,
+    owner_hbm,
+    target_hbm,
     vectors_hbm,
     leaf_hbm,
     src_hbm,
@@ -38,6 +38,11 @@
     tgt_hbm,
     out_basis_hbm,
     out_ref,
+    src_pair,
+    tgt_pair,
+    sources,
+    owner,
+    target,
     vectors,
     leaf,
     src,
@@ -54,15 +59,17 @@
     table_vmem,
     table,
     running,
-    dense,
-    arrived,
+    dense_a,
+    dense_b,
+    arrived_a,
+    arrived_b,
     load_sem,
     table_sem,
     send_sem,
     recv_sem,
 ):
     me = lax.axis_index("leaf")
-    bits = len(order_of_bits)
+    bits = len(orders[0])
     blocks = leaf.shape[0]
     halves = blocks // 2
     pairs = pair.shape[0]
@@ -77,7 +84,12 @@
             [
                 (vectors_hbm, vectors),
                 (leaf_hbm, leaf),
+                (src_pair_hbm, src_pair),
                 (src_hbm, src),
+                (sources_hbm, sources),
+                (owner_hbm, owner),
+                (target_hbm, target),
+                (tgt_pair_hbm, tgt_pair),
                 (src_cross_hbm, src_cross),
                 (pair_hbm, pair),
                 (tgt_cross_hbm, tgt_cross),
@@ -134,6 +146,7 @@
     for b in range(blocks):
         state_a[b] = twice(vectors[:, b * points : (b + 1) * points], leaf[b]).astype(BF16)
     loads[2].wait()
+    loads[3].wait()
     now, later = state_a, state_b
     for depth in range(levels):
         local_level(src, depth, src_pair, now, later)
@@ -148,18 +161,27 @@
     count_shape = (pairs, pairs)
     item = lax.broadcasted_iota(I32, count_shape, 0)
     lane = lax.broadcasted_iota(I32, count_shape, 1)
-    key = jnp.broadcast_to(owner[...] * blocks + target[...], count_shape)
-    first = jnp.broadcast_to(sources[:, 0:1], count_shape)
-    second = jnp.broadcast_to(sources[:, 1:2], count_shape)
-    key_row = jnp.sum(jnp.where(item == lane, key, 0), axis=0, keepdims=True)
+    for load in loads[4:8]:
+        load.wait()
+    key_row = owner[...] * blocks + target[...]
+    tag_row = (key_row * blocks + sources[0:1, :]) * blocks + sources[1:2, :]
+    tag = jnp.sum(jnp.where(item == lane, tag_row, 0), axis=1, keepdims=True)
+    tag = jnp.broadcast_to(tag, count_shape)
+    key = tag // (blocks * blocks)
     before = jnp.where((key_row == key) & (lane < item), 1, 0)
     smaller = jnp.where(key_row < key, 1, 0)
     place = jnp.sum(before + smaller, axis=1, keepdims=True)
     follows = jnp.minimum(jnp.sum(before, axis=1, keepdims=True), 1)
     sits = place == lane
+    fields = [
+        jnp.sum(jnp.where(sits, value, 0), axis=0, keepdims=True)
+        for value in (item, tag, jnp.broadcast_to(follows, count_shape))
+    ]
     rows = [
-        jnp.sum(jnp.where(sits, value, 0), axis=0, keepdims=True)
-        for value in (item, first, second, jnp.broadcast_to(follows, count_shape))
+        fields[0],
+        (fields[1] // blocks) % blocks,
+        fields[1] % blocks,
+        fields[2],
     ]
     for r in range(4):
         table_vmem[r : r + 1, :] = rows[r]
@@ -173,11 +195,11 @@
     to_scalars = pltpu.make_async_copy(table_vmem, table, table_sem)
     to_scalars.start()
     running[pairs] = jnp.zeros((vec, width), BF16)
-    loads[3].wait()
-    loads[4].wait()
+    loads[8].wait()
+    loads[9].wait()
     to_scalars.wait()
 
-    cross.wait()
+    cross.wait_recv()
     cross_level(src_cross, now, cross_in, later)
     now, later = later, now
 
@@ -194,49 +216,82 @@
 
     lax.fori_loop(0, pairs // group, interactions, jnp.zeros((vec, width), F32))
 
-    def place_owner(position, carry):
-        who = 0
-        for s, bit in enumerate(order_of_bits):
-            away = bit_of(position, bits - 1 - s)
-            who = who + ((bit_of(me, bit) + away) % 2) * (1 << bit)
-        start = who * blocks
-        row = 4 + start // pairs
-        column = start % pairs
-        for j in range(halves):
-            one = running[table[row, column + 2 * j]]
-            two = running[table[row, column + 2 * j + 1]]
-            dense[position * halves + j] = jnp.where(low, one, two)
-        return carry
-
-    lax.fori_loop(0, devices, place_owner, 0)
-
-    unit = 8
-    for s, bit in enumerate(order_of_bits):
-        size = (devices >> (s + 1)) * halves
-        part = arrived.at[size : 2 * size]
-        move = send(dense.at[size : 2 * size], part, bit, 1 + s)
-        move.start()
-        move.wait()
-
-        def add(step, carry):
+    half = vec // 2
+    dense = (dense_a, dense_b)
+    arrived = (arrived_a, arrived_b)
+
+    def place(h, begin, end):
+        part = pl.ds(h * half, half)
+        low_half = low[:half]
+
+        def place_owner(position, carry):
+            who = 0
+            for s, bit in enumerate(orders[h]):
+                away = bit_of(position, bits - 1 - s)
+                who = who + ((bit_of(me, bit) + away) % 2) * (1 << bit)
+            start = who * blocks
+            row = 4 + start // pairs
+            column = start % pairs
+            for j in range(halves):
+                one = running[table[row, column + 2 * j], part, :]
+                two = running[table[row, column + 2 * j + 1], part, :]
+                dense[h][position * halves + j] = jnp.where(low_half, one, two)
+            return carry
+
+        lax.fori_loop(begin, end, place_owner, 0)
+
+    unit = 4
+
+    def add(h, offset, begin, end):
+        def step_of(step, carry):
             for u in range(unit):
                 k = step * unit + u
-                dense[k] = (dense[k].astype(F32) + arrived[size + k].astype(F32)).astype(BF16)
+                total = dense[h][k].astype(F32) + arrived[h][offset + k].astype(F32)
+                dense[h][k] = total.astype(BF16)
             return carry
 
-        lax.fori_loop(0, size // unit, add, 0)
-
-    near = send(dense.at[0:halves], near_in, 0, 1 + bits)
+        lax.fori_loop(begin // unit, end // unit, step_of, 0)
+
+    def move_of(h, s):
+        size = (devices >> (s + 1)) * halves
+        part = pl.ds(size, size)
+        slot = 2 + 2 * s + h
+        return send(dense[h].at[part], arrived[h].at[part], orders[h][s], slot)
+
+    moves = [[move_of(h, s) for s in range(bits)] for h in range(2)]
+    for h in range(2):
+        place(h, devices // 2, devices)
+        moves[h][0].start()
+    for h in range(2):
+        place(h, 0, devices // 2)
+    for s in range(bits):
+        size = (devices >> (s + 1)) * halves
+        for h in range(2):
+            moves[h][s].wait_recv()
+            if s + 1 < bits:
+                add(h, size, size // 2, size)
+                moves[h][s + 1].start()
+                add(h, size, 0, size // 2)
+            else:
+                add(h, size, 0, size)
+    middle = packed
+    cross.wait_send()
+    for j in range(halves):
+        middle[j] = jnp.concatenate([dense_a[j], dense_b[j]], axis=0)
+
+    near = send(middle, near_in, 0, 1)
     near.start()
     for j in range(halves):
-        x = dense[j]
+        x = middle[j]
         later[2 * j] = jnp.concatenate([x[:, :rank], x[:, :rank]], axis=1)
         later[2 * j + 1] = jnp.concatenate([x[:, rank:], x[:, rank:]], axis=1)
     now, later = later, now
-    loads[5].wait()
-    loads[6].wait()
-    loads[7].wait()
+    for load in loads[10:]:
+        load.wait()
     near.wait()
+    for h in range(2):
+        for move in moves[h]:
+            move.wait_send()
     cross_level(tgt_cross, now, near_in, later)
     now, later = later, now
     for depth in range(levels):
@@ -271,6 +326,13 @@
     width = 2 * rank
     rows = 4 + devices * blocks // pairs
     rows = -(-rows // 8) * 8
+    small = [
+        src_pairing,
+        tgt_pairing,
+        pair_sources.T,
+        pair_owner.reshape(1, pairs),
+        pair_target.reshape(1, pairs),
+    ]
     big = [
         vectors,
         leaf_basis,
@@ -282,14 +344,16 @@
         out_basis,
     ]
     vmem = pl.BlockSpec(memory_space=pltpu.VMEM)
-    smem = pl.BlockSpec(memory_space=pltpu.SMEM)
-    hbm = pl.BlockSpec(memory_space=pl.ANY)
+    hbm = pl.BlockSpec(memory_space=pltpu.HBM)
+    rest = list(range(1, bits))
+    orders = ([0] + rest, [0] + rest[len(rest) // 2 :] + rest[: len(rest) // 2])
     return pl.pallas_call(
-        functools.partial(kernel, devices, tuple(range(bits))),
+        functools.partial(kernel, devices, orders),
         out_shape=jax.ShapeDtypeStruct(vectors.shape, BF16),
-        in_specs=[smem, smem, vmem, vmem, vmem] + [hbm] * len(big),
+        in_specs=[hbm] * (len(small) + len(big)),
         out_specs=vmem,
-        scratch_shapes=[pltpu.VMEM(a.shape, a.dtype) for a in big]
+        scratch_shapes=[pltpu.SMEM(a.shape, I32) for a in small[:2]]
+        + [pltpu.VMEM(a.shape, a.dtype) for a in small[2:] + big]
         + [
             pltpu.VMEM((blocks, vec, width), BF16),
             pltpu.VMEM((blocks, vec, width), BF16),
@@ -299,22 +363,20 @@
             pltpu.VMEM((rows, pairs), I32),
             pltpu.SMEM((rows, pairs), I32),
             pltpu.VMEM((pairs + 1, vec, width), BF16),
-            pltpu.VMEM((devices * halves, vec, width), BF16),
-            pltpu.VMEM((devices * halves, vec, width), BF16),
-            pltpu.SemaphoreType.DMA((len(big),)),
+            pltpu.VMEM((devices * halves, vec // 2, width), BF16),
+            pltpu.VMEM((devices * halves, vec // 2, width), BF16),
+            pltpu.VMEM((devices * halves, vec // 2, width), BF16),
+            pltpu.VMEM((devices * halves, vec // 2, width), BF16),
+            pltpu.SemaphoreType.DMA((len(small) + len(big),)),
             pltpu.SemaphoreType.DMA,
-            pltpu.SemaphoreType.DMA((2 + bits,)),
-            pltpu.SemaphoreType.DMA((2 + bits,)),
+            pltpu.SemaphoreType.DMA((2 + 2 * bits,)),
+            pltpu.SemaphoreType.DMA((2 + 2 * bits,)),
         ],
         compiler_params=pltpu.CompilerParams(
-            collective_id=0, has_side_effects=True, vmem_limit_bytes=48 * 1024 * 1024
+            collective_id=0, has_side_effects=True, vmem_limit_bytes=63 * 1024 * 1024
         ),
     )(
-        src_pairing,
-        tgt_pairing,
-        pair_sources,
-        pair_owner,
-        pair_target.reshape(pairs, 1),
+        *small,
         *big,
     )
 

time: 49.9 us -> 34.6 us (0.69)
  local copies, waits for them, and re-layouts: 12.9 us -> 1.57 us
  Pallas kernels: 36.5 us -> 32.9 us
    unnamed x23 -> x1, local copies, waits for them, and re-layouts: 12.1 us -> 1.57 us
    pallas_call x1, Pallas kernels: 36.5 us -> 32.9 us  [body(): pl.pallas_call(functools.partial(kernel, devices, orders), out_shape=jax....]
    reshape x1 -> x0, local copies, waits for them, and re-layouts: 0.76 us -> none  [body(): pair_target.reshape(pairs, 1)]
where the time goes in v2:
time: 34.6 us; the launch traced here: 34.5 us
  Pallas kernels  32.9 us (95%)
  local copies, waits for them, and re-layouts  1.57 us (5%)
    pallas_call x1, Pallas kernels, body(): pl.pallas_call(functools.partial(kernel, devices, orders), out_shape=jax....  32.9 us
    unnamed x1, local copies, waits for them, and re-layouts  1.57 us

profile of v2, /device:TPU:0, one launch (start us, length us, event | category | flops | bytes accessed | tf_op | source)
XLA Modules:
  0.0 34.5 jit_solution(1965412958936347666)
XLA Ops:
  0.0 32.9 %shard_map.127 = bf16[32,2048]{1,0:T(8,128)(2,1)} custom-call(s32[3,16]{1,0:T(4,128)} %src_pair_hbm.1, s32[3,16]{1,0:T(4,128)} %tgt_pair_hbm.1, s32[2,128]{1,0:T(2,128)} %bitcast.3, s32[1,128]{1,0:T(1,128)} %bitcast.4, s32[1,128]{1,0:T(1,128)} %bitcast.5, bf16[32,2048]{1,0:T(8,128)(2,1)} %vectors_hbm.1, bf16[16,64,128]{2,1,0:T(8,128)(2,1)} %leaf_hbm.1, ...), custom_call_target="tpu_custom_call" | custom-call | tf_op jit(solution)/shard_map/pallas_call | solution.py:350
  32.9 1.6 %copy.15 = bf16[32,2048]{1,0:T(8,128)(2,1)} copy(bf16[32,2048]{1,0:T(8,128)(2,1)} %shard_map.127) | data formatting | bytes 262144

commit v3 on v2

--- a/solution.py
+++ b/solution.py
@@ -122,14 +122,17 @@
 
     low = lax.broadcasted_iota(I32, (vec, width), 1) < rank
 
-    def twice(x, factor):
-        both = jnp.concatenate([factor, factor], axis=0)
-        return lax.dot_general(x, both, NT, preferred_element_type=F32)
+    def times(x, factor):
+        return lax.dot_general(x, factor, NT, preferred_element_type=F32)
+
+    def twice(y):
+        y = y.astype(BF16)
+        return jnp.concatenate([y, y], axis=1)
 
     def local_level(factors, depth, pairing, old, new):
         for b in range(blocks):
             x = jnp.where(low, old[b], old[pairing[depth, b]])
-            new[b] = twice(x, factors[depth, b]).astype(BF16)
+            new[b] = twice(times(x, factors[depth, b]))
 
     def cross_level(factors, own, other, new):
         for b in range(blocks):
@@ -138,13 +141,13 @@
                 x = jnp.concatenate([x[:, rank:], x[:, :rank]], axis=1)
             else:
                 x = jnp.where(low, own[b], other[b // 2])
-            new[b] = twice(x, factors[b]).astype(BF16)
+            new[b] = twice(times(x, factors[b]))
 
     loads[0].wait()
     loads[1].wait()
     points = leaf.shape[2]
     for b in range(blocks):
-        state_a[b] = twice(vectors[:, b * points : (b + 1) * points], leaf[b]).astype(BF16)
+        state_a[b] = twice(times(vectors[:, b * points : (b + 1) * points], leaf[b]))
     loads[2].wait()
     loads[3].wait()
     now, later = state_a, state_b
@@ -203,39 +206,40 @@
     cross_level(src_cross, now, cross_in, later)
     now, later = later, now
 
-    group = 16
+    group = 128
 
     def interactions(step, total):
         for k in range(group):
             i = step * group + k
             x = jnp.where(low, now[table[1, i]], now[table[2, i]])
-            c = twice(x, pair[table[0, i]]).astype(BF16).astype(F32)
+            c = times(x, pair[table[0, i]]).astype(BF16).astype(F32)
             total = total * table[3, i].astype(F32) + c
-            running[i] = total.astype(BF16)
+            running[i] = twice(total)
         return total
 
-    lax.fori_loop(0, pairs // group, interactions, jnp.zeros((vec, width), F32))
+    lax.fori_loop(0, pairs // group, interactions, jnp.zeros((vec, rank), F32))
 
     half = vec // 2
     dense = (dense_a, dense_b)
     arrived = (arrived_a, arrived_b)
 
-    def place(h, begin, end):
-        part = pl.ds(h * half, half)
-        low_half = low[:half]
-
+    def place(begin, end):
         def place_owner(position, carry):
-            who = 0
-            for s, bit in enumerate(orders[h]):
+            who, spots = 0, [0, 0]
+            for s, bit in enumerate(orders[0]):
                 away = bit_of(position, bits - 1 - s)
                 who = who + ((bit_of(me, bit) + away) % 2) * (1 << bit)
+                for h in range(2):
+                    spots[h] += away * (1 << (bits - 1 - orders[h].index(bit)))
             start = who * blocks
             row = 4 + start // pairs
             column = start % pairs
             for j in range(halves):
-                one = running[table[row, column + 2 * j], part, :]
-                two = running[table[row, column + 2 * j + 1], part, :]
-                dense[h][position * halves + j] = jnp.where(low_half, one, two)
+                one = running[table[row, column + 2 * j]]
+                two = running[table[row, column + 2 * j + 1]]
+                both = jnp.where(low, one, two)
+                dense_a[spots[0] * halves + j] = both[:half]
+                dense_b[spots[1] * halves + j] = both[half:]
             return carry
 
         lax.fori_loop(begin, end, place_owner, 0)
@@ -259,21 +263,20 @@
         return send(dense[h].at[part], arrived[h].at[part], orders[h][s], slot)
 
     moves = [[move_of(h, s) for s in range(bits)] for h in range(2)]
+    place(devices // 2, devices)
     for h in range(2):
-        place(h, devices // 2, devices)
         moves[h][0].start()
-    for h in range(2):
-        place(h, 0, devices // 2)
+    place(0, devices // 2)
     for s in range(bits):
         size = (devices >> (s + 1)) * halves
         for h in range(2):
             moves[h][s].wait_recv()
+            add(h, size, size // 2 if s + 1 < bits else 0, size)
             if s + 1 < bits:
-                add(h, size, size // 2, size)
                 moves[h][s + 1].start()
+        if s + 1 < bits:
+            for h in range(2):
                 add(h, size, 0, size // 2)
-            else:
-                add(h, size, 0, size)
     middle = packed
     cross.wait_send()
     for j in range(halves):

time: 34.6 us -> 32.6 us (0.942)
  Pallas kernels: 32.9 us -> 30.8 us
    pallas_call x1, Pallas kernels: 32.9 us -> 30.8 us  [body(): pl.pallas_call(functools.partial(kernel, devices, orders), out_shape=jax....]
where the time goes in v3:
time: 32.6 us; the launch traced here: 32.4 us
  Pallas kernels  30.8 us (94%)
  local copies, waits for them, and re-layouts  1.57 us (5%)
    pallas_call x1, Pallas kernels, body(): pl.pallas_call(functools.partial(kernel, devices, orders), out_shape=jax....  30.8 us
    unnamed x1, local copies, waits for them, and re-layouts  1.57 us

profile of v3, /device:TPU:0, one launch (start us, length us, event | category | flops | bytes accessed | tf_op | source)
XLA Modules:
  0.0 32.4 jit_solution(4285322960290809335)
XLA Ops:
  0.0 30.8 %shard_map.127 = bf16[32,2048]{1,0:T(8,128)(2,1)} custom-call(s32[3,16]{1,0:T(4,128)} %src_pair_hbm.1, s32[3,16]{1,0:T(4,128)} %tgt_pair_hbm.1, s32[2,128]{1,0:T(2,128)} %bitcast.3, s32[1,128]{1,0:T(1,128)} %bitcast.4, s32[1,128]{1,0:T(1,128)} %bitcast.5, bf16[32,2048]{1,0:T(8,128)(2,1)} %vectors_hbm.1, bf16[16,64,128]{2,1,0:T(8,128)(2,1)} %leaf_hbm.1, ...), custom_call_target="tpu_custom_call" | custom-call | tf_op jit(solution)/shard_map/pallas_call | solution.py:353
  30.9 1.6 %copy.15 = bf16[32,2048]{1,0:T(8,128)(2,1)} copy(bf16[32,2048]{1,0:T(8,128)(2,1)} %shard_map.127) | data formatting | bytes 262144

commit v4 on v3

--- a/solution.py
+++ b/solution.py
@@ -223,12 +223,14 @@
     dense = (dense_a, dense_b)
     arrived = (arrived_a, arrived_b)
 
+    mine = [bit_of(me, bit) for bit in range(bits)]
+
     def place(begin, end):
         def place_owner(position, carry):
             who, spots = 0, [0, 0]
             for s, bit in enumerate(orders[0]):
                 away = bit_of(position, bits - 1 - s)
-                who = who + ((bit_of(me, bit) + away) % 2) * (1 << bit)
+                who = who + (mine[bit] + away - 2 * mine[bit] * away) * (1 << bit)
                 for h in range(2):
                     spots[h] += away * (1 << (bits - 1 - orders[h].index(bit)))
             start = who * blocks
@@ -242,7 +244,11 @@
                 dense_b[spots[1] * halves + j] = both[half:]
             return carry
 
-        lax.fori_loop(begin, end, place_owner, 0)
+        if devices > 16:
+            lax.fori_loop(begin, end, place_owner, 0)
+        else:
+            for position in range(begin, end):
+                place_owner(position, 0)
 
     unit = 4
 

time: 32.6 us -> 32.1 us (0.985)
  Pallas kernels: 30.8 us -> 30.4 us
    pallas_call x1, Pallas kernels: 30.8 us -> 30.4 us  [body(): pl.pallas_call(functools.partial(kernel, devices, orders), out_shape=jax....]
where the time goes in v4:
time: 32.1 us; the launch traced here: 32 us
  Pallas kernels  30.4 us (95%)
  local copies, waits for them, and re-layouts  1.57 us (5%)
    pallas_call x1, Pallas kernels, body(): pl.pallas_call(functools.partial(kernel, devices, orders), out_shape=jax....  30.4 us
    unnamed x1, local copies, waits for them, and re-layouts  1.57 us

profile of v4, /device:TPU:0, one launch (start us, length us, event | category | flops | bytes accessed | tf_op | source)
XLA Modules:
  0.0 32.0 jit_solution(16506360378392283562)
XLA Ops:
  0.0 30.4 %shard_map.127 = bf16[32,2048]{1,0:T(8,128)(2,1)} custom-call(s32[3,16]{1,0:T(4,128)} %src_pair_hbm.1, s32[3,16]{1,0:T(4,128)} %tgt_pair_hbm.1, s32[2,128]{1,0:T(2,128)} %bitcast.3, s32[1,128]{1,0:T(1,128)} %bitcast.4, s32[1,128]{1,0:T(1,128)} %bitcast.5, bf16[32,2048]{1,0:T(8,128)(2,1)} %vectors_hbm.1, bf16[16,64,128]{2,1,0:T(8,128)(2,1)} %leaf_hbm.1, ...), custom_call_target="tpu_custom_call" | custom-call | tf_op jit(solution)/shard_map/pallas_call | solution.py:359
  30.4 1.6 %copy.15 = bf16[32,2048]{1,0:T(8,128)(2,1)} copy(bf16[32,2048]{1,0:T(8,128)(2,1)} %shard_map.127) | data formatting | bytes 262144
